TPU v7x, 1024 devices: a whole 4x4x32 slice. The times are simulated.
1024 devices in a mesh: dp: 8 (over z_hi, y), expert: 64 (over x, z_lo), tensor: 2 (over core).
Axes of the slice: x: 4, y: 4, z: 32 (z_hi: 2, z_lo: 16; z = z_hi * 16 + z_lo), core: 2. Of those that a mesh axis runs over, the one named last changes fastest.
Arguments:
- layer_input: bfloat16 [8192, 7168], P('expert'), may hold values from -0.875 to 0.875
- routes: int32 [8192, 2], P('expert'), may hold values from 0 to 31, all different within a row; in each aligned block of 128 rows (0 to 127, 128 to 255, ...) at most 12 rows name the same one
- dense_cot: bfloat16 [8192, 2560], P('expert', ('dp', 'tensor')), may hold values from -1.5 to 1.5
- dense_weight: bfloat16 [7168, 2560], P(None, ('dp', 'tensor')), may hold values from -0.125 to 0.125
- expert_cot: bfloat16 [768, 81920], P(None, 'expert'), may hold values from -6 to 6
- expert_weight: bfloat16 [7168, 81920], P(('dp', 'tensor'), 'expert'), may hold values from -0.125 to 0.125
Outputs:
- input_grad: bfloat16 [8192, 7168], P('expert', ('dp', 'tensor'))
- dense_wgrad: float32 [7168, 2560], P('expert', ('dp', 'tensor'))
- expert_wgrad: bfloat16 [7168, 81920], P(('dp', 'tensor'), 'expert')
Inputs may be any that keep to these rules, and one draw needn't show every extreme that they name: `routes`: the two experts of a token differ. Among the 128 tokens of one device no expert is named more than 12 times, and in every draw some device names some expert exactly 12 times.
All inputs are finite; a program needn't handle non-finite values.
Results may differ from a plain program's by a relative error of at most 0.0065.
Values may be sent and summed in bfloat16 or wider, within the bound.
A program may use at most 64 MiB of HBM per device.

v0:
```python
import jax
import jax.numpy as jnp
from jax import lax
from jax.sharding import PartitionSpec as P


def contract_rows(left, right):
    return lax.dot_general(
        left, right, (((0,), (0,)), ((), ())), preferred_element_type=jnp.float32
    )


def contract_cols(left, right):
    return lax.dot_general(
        left, right, (((1,), (1,)), ((), ())), preferred_element_type=jnp.float32
    )


def body(layer_input, routes, dense_cot, dense_weight, expert_cot, expert_weight):
    expert_devices = lax.axis_size("expert")
    expert_count = expert_devices // 2
    token_rows = layer_input.shape[0]
    feat_dev = expert_weight.shape[0]
    capacity = expert_cot.shape[0] // expert_devices
    group_index = lax.axis_index(("dp", "tensor"))
    feature_slice = lax.dynamic_slice_in_dim(layer_input, group_index * feat_dev, feat_dev, 1)
    flat_routes = routes.reshape(-1)
    onehot = (flat_routes[:, None] == jnp.arange(expert_count, dtype=jnp.int32)[None, :]).astype(
        jnp.int32
    )
    earlier = jnp.cumsum(onehot, axis=0) - onehot
    slot_rank = jnp.sum(earlier * onehot, axis=1)
    targets = (flat_routes * capacity + slot_rank).reshape(token_rows, 2)
    slot_ids = jnp.arange(expert_count * capacity, dtype=jnp.int32)
    dispatch = jnp.sum(
        (slot_ids[:, None, None] == targets[None, :, :]).astype(jnp.int32), axis=2
    ).astype(jnp.bfloat16)
    outgoing = jnp.dot(dispatch, feature_slice, preferred_element_type=jnp.float32).astype(
        jnp.bfloat16
    )
    outgoing = jnp.broadcast_to(
        outgoing.reshape(expert_count, 1, capacity, feat_dev), (expert_count, 2, capacity, feat_dev)
    ).reshape(expert_devices, capacity, feat_dev)
    received = lax.all_to_all(outgoing, "expert", split_axis=0, concat_axis=0, tiled=True).reshape(
        expert_devices * capacity, feat_dev
    )
    expert_wgrad = contract_rows(received, expert_cot).astype(jnp.bfloat16)
    partial_rows = contract_cols(expert_cot, expert_weight).astype(jnp.bfloat16)
    partial_rows = partial_rows.reshape(expert_devices, capacity, feat_dev)
    returned = lax.all_to_all(
        partial_rows, "expert", split_axis=0, concat_axis=0, tiled=True
    ).reshape(expert_count, 2, capacity, feat_dev)
    lower_half = returned[:, 0].reshape(expert_count * capacity, feat_dev)
    upper_half = returned[:, 1].reshape(expert_count * capacity, feat_dev)
    expert_sum = contract_rows(dispatch, lower_half) + contract_rows(dispatch, upper_half)
    dense_partial = contract_cols(dense_cot, dense_weight)
    dense_sum = lax.psum_scatter(
        dense_partial.astype(jnp.bfloat16), ("dp", "tensor"), scatter_dimension=1, tiled=True
    ).astype(jnp.float32)
    input_grad = (dense_sum + expert_sum).astype(jnp.bfloat16)
    dense_wgrad = lax.psum_scatter(
        contract_rows(layer_input, dense_cot), "expert", scatter_dimension=0, tiled=True
    )
    return (input_grad, dense_wgrad, expert_wgrad)


def solution(mesh):
    placed = (
        P("expert", None),
        P("expert", None),
        P("expert", ("dp", "tensor")),
        P(None, ("dp", "tensor")),
        P(None, "expert"),
        P(("dp", "tensor"), "expert"),
    )
    return jax.shard_map(
        body,
        mesh=mesh,
        in_specs=placed,
        out_specs=(
            P("expert", ("dp", "tensor")),
            P("expert", ("dp", "tensor")),
            P(("dp", "tensor"), "expert"),
        ),
        check_vma=False,
    )
```

profile of v0, /device:TPU:24, one launch (start us, length us, event | category | flops | bytes accessed | tf_op | source)
XLA Modules:
  0.0 1074.7 jit_solution(4850982318179194088)
XLA Ops:
  7.2 1.6 copy-done
  8.8 3.6 convolution_convert_fusion
  12.5 3.8 convolution_convert_fusion.2
  16.3 1.4 copy.43
  17.7 1.2 reshape.45
  18.9 29.2 %all-to-all-start = ((bf16[64,12,448]{2,1,0:T(8,128)(2,1)}), bf16[64,12,448]{2,1,0:T(8,128)(2,1)S(1)}, u32[]{:S(2)}, u32[]{:S(2)}) async-start(bf16[64,12,448]{2,1,0:T(8,128)(2,1)} %reshape.45), calls=%async_computation.1 | async-start | bytes 2097152 | tf_op jit(solution)/shard_map/all_to_all | solution.py:50
  48.2 5.7 fusion.12
  53.9 0.7 copy-done.3
  56.2 2.1 convolution_convert_fusion.3
  58.3 1.9 copy.46
  60.2 1.9 broadcast_in_dim.4
  62.1 124.6 %all-to-all-done = bf16[64,12,448]{2,1,0:T(8,128)(2,1)S(1)} async-done(((bf16[64,12,448]{2,1,0:T(8,128)(2,1)}), bf16[64,12,448]{2,1,0:T(8,128)(2,1)S(1)}, u32[]{:S(2)}, u32[]{:S(2)}) %all-to-all-start) | async-done | bytes 688160 | tf_op jit(solution)/shard_map/all_to_all | solution.py:50
  186.7 2.5 broadcast_in_dim.10
  189.2 13.2 %all-to-all-start.1 = ((bf16[64,12,448]{2,1,0:T(8,128)(2,1)}), bf16[64,12,448]{2,1,0:T(8,128)(2,1)S(1)}, u32[]{:S(2)}, u32[]{:S(2)}) async-start(bf16[64,12,448]{2,1,0:T(8,128)(2,1)} %bitcast.41), calls=%async_computation.2 | async-start | bytes 2097152 | tf_op jit(solution)/shard_map/all_to_all | solution.py:44
  202.5 2.2 slice_bitcast_fusion
  204.7 2.0 reshape_squeeze.6
  206.7 2.0 reshape_squeeze.7
  208.7 108.8 %all-to-all-done.1 = bf16[64,12,448]{2,1,0:T(8,128)(2,1)S(1)} async-done(((bf16[64,12,448]{2,1,0:T(8,128)(2,1)}), bf16[64,12,448]{2,1,0:T(8,128)(2,1)S(1)}, u32[]{:S(2)}, u32[]{:S(2)}) %all-to-all-start.1) | async-done | bytes 688160 | tf_op jit(solution)/shard_map/all_to_all | solution.py:44
  317.5 1.3 reshape.48
  318.8 1.3 fusion.10
  320.1 2.0 fusion.1
  322.1 3.9 convolution_convert_fusion.1
  326.0 740.2 %reduce-scatter.7.cloned.1.call-done = f32[112,160]{1,0:T(8,128)} async-done(((f32[7168,160]{1,0:T(8,128)}), f32[112,160]{1,0:T(8,128)}) %reduce-scatter.7.cloned.1.call-update) | async-done | bytes 71696
  1066.2 1.6 copy.48
  (24 shorter events, 1.7 us)
Async XLA Ops:
  7.2 1.7 copy-start
  7.2 312.9 %reduce-scatter.5.cloned.1.call-start = ((), (), s32[]{:S(2)}) async-start(), calls=%async_computation.4 | async-start | bytes 1949696 | tf_op jit(solution)/shard_map/reduce_scatter | solution.py:57
  17.7 30.5 %copy-start.2 = (bf16[128,160]{0,1:T(8,128)(2,1)S(1)}, bf16[128,160]{0,1:T(8,128)(2,1)}, u32[]{:S(2)}) copy-start(bf16[128,160]{0,1:T(8,128)(2,1)} %param.8) | copy-start | bytes 122884
  18.9 167.8 %all-to-all-start = ((bf16[64,12,448]{2,1,0:T(8,128)(2,1)}), bf16[64,12,448]{2,1,0:T(8,128)(2,1)S(1)}, u32[]{:S(2)}, u32[]{:S(2)}) async-start(bf16[64,12,448]{2,1,0:T(8,128)(2,1)} %reshape.45), calls=%async_computation.1 | async-start | bytes 2097152 | tf_op jit(solution)/shard_map/all_to_all | solution.py:50
  48.1 1018.0 %reduce-scatter.7.cloned.1.call-start = ((), (), s32[]{:S(2)}) async-start(), calls=%async_computation.5 | async-start | bytes 7454720
  53.9 0.7 copy-start.3
  186.7 2.5 copy-start.1
  189.2 128.3 %all-to-all-start.1 = ((bf16[64,12,448]{2,1,0:T(8,128)(2,1)}), bf16[64,12,448]{2,1,0:T(8,128)(2,1)S(1)}, u32[]{:S(2)}, u32[]{:S(2)}) async-start(bf16[64,12,448]{2,1,0:T(8,128)(2,1)} %bitcast.41), calls=%async_computation.2 | async-start | bytes 2097152 | tf_op jit(solution)/shard_map/all_to_all | solution.py:44
Sparse Core Ops, SparseCore 0:
  14.0 229.0 reduce-scatter.4
  246.9 819.2 reduce-scatter.6
where the time goes:
time: 1080 us; the launch traced here: 1070 us
  waiting for transfers between devices  974 us (90%)
  starting transfers between devices  42.6 us (4%)
  matrix products  22.4 us (2%)
  local copies, waits for them, and re-layouts  21.1 us (2%)
  between operations  14.1 us (1%)
    unnamed x3, waiting for transfers between devices  740 us
    all_to_all x1, waiting for transfers between devices, body(): lax.all_to_all(partial_rows, 'expert', split_axis=0, concat_axis=0, tiled...  125 us
    all_to_all x1, waiting for transfers between devices, body(): lax.all_to_all(outgoing, 'expert', split_axis=0, concat_axis=0, tiled=True)  109 us
    all_to_all x1, starting transfers between devices, body(): lax.all_to_all(partial_rows, 'expert', split_axis=0, concat_axis=0, tiled...  29.2 us
  transfers between devices with their start and end apart: 4, of which 3 were waited for; matrix products, arithmetic and copies ran while one was open for 3% of the time, Pallas kernels for 0%

commit v1 on v0

v1 whole, which is shorter than its diff:
```python
import functools

import jax
import jax.numpy as jnp
import numpy as np
from jax import lax
from jax.experimental import pallas as pl
from jax.experimental.pallas import tpu as pltpu
from jax.sharding import PartitionSpec as P

MESH = pl.DeviceIdType.MESH
F32 = jnp.float32
BF16 = jnp.bfloat16
CAP = 12
NX, NY = 4, 4


def dot(a, b, ca, cb):
    return lax.dot_general(a, b, (((ca,), (cb,)), ((), ())), preferred_element_type=F32)


def rev_bits(q, bits):
    return sum(((q >> b) & 1) << (bits - 1 - b) for b in range(bits))


def up(n, m):
    return -(-n // m) * m


def kernel(
    dims,
    li, rt, cot, wt, ecot, ew, p_x, p_z, e_mat, m_mat,
    o_in, o_dw, o_ew,
    dmat, xs, xr, zs, zr, prt, pz, pin, rs, rz, qs, rx,
    dacc, dsend, dcore, ysend, yrecv, hsend, hrecv,
    wxs, wxr, wz, wzr,
    dx_s, dx_r, dz_s, dz_r, df_s, df_r, pe_s, pe_r, rz_s, rz_r, rx_s, rx_r,
    c_s, c_r, y_s, y_r, h_s, h_r, wx_s, wx_r, wz_s, wz_r,
):
    nx, nz, ny, nh = dims
    pairs = nz // 2
    bits = nz.bit_length() - 1
    feat = ew.shape[0]
    fpad = xs.shape[2]
    wl = o_dw.shape[1]
    win_w = nz * wl
    rowx = pairs * CAP
    dp = lax.axis_index("dp")
    ex = lax.axis_index("expert")
    core = lax.axis_index("tensor")
    x, z = ex // nz, ex % nz
    zh, y = dp // ny, dp % ny
    pair, par = z // 2, z % 2

    def at_x(d):
        return (dp, lax.rem(x + d, nx) * nz + z, core)

    def at_z(zz):
        return (dp, x * nz + zz, core)

    def at_pair(d):
        return at_z(lax.rem(pair + d, pairs) * 2 + par)

    beside = at_z(z + 1 - 2 * par)
    other_core = (dp, ex, 1 - core)

    def at_y(d):
        return (zh * ny + lax.rem(y + d, ny), ex, core)

    other_h = ((1 - zh) * ny + y, ex, core)

    def copy(src, dst, send, recv, dev):
        return pltpu.make_async_remote_copy(
            src_ref=src, dst_ref=dst, send_sem=send, recv_sem=recv,
            device_id=dev, device_id_type=MESH,
        )

    met = [at_x(d) for d in range(1, nx)] + [at_pair(d) for d in range(1, pairs)]
    met += [beside, other_core] + [at_y(d) for d in range(1, ny)] + [other_h]
    barrier = pltpu.get_barrier_semaphore()
    for dev in met:
        pl.semaphore_signal(barrier, inc=1, device_id=dev, device_id_type=MESH)

    r = rt[...]
    e_row = lax.broadcasted_iota(jnp.int32, (e_mat.shape[1], r.shape[1]), 0)
    member = ((e_row == r[0:1, :]) | (e_row == r[1:2, :])).astype(F32).astype(BF16)
    n_tok = r.shape[1]
    before = lax.broadcasted_iota(jnp.int32, (n_tok, n_tok), 0) < lax.broadcasted_iota(
        jnp.int32, (n_tok, n_tok), 1
    )
    rank = dot(member, before.astype(F32).astype(BF16), 1, 0).astype(BF16)
    is_member = dot(e_mat[...], member, 1, 0)
    ranks = dot(e_mat[...], rank, 1, 0)
    dmat[...] = ((is_member > 0.5) & (ranks == m_mat[...])).astype(F32).astype(BF16)
    chip_w = 2 * feat
    window = li[:, pl.ds(pl.multiple_of(dp * chip_w, 128), chip_w)]
    pick_r = lax.broadcasted_iota(jnp.int32, (chip_w, fpad), 0)
    pick_c = lax.broadcasted_iota(jnp.int32, (chip_w, fpad), 1)
    pick = ((pick_r == pick_c + core * feat) & (pick_c < feat)).astype(F32).astype(BF16)
    mine = dot(window, pick, 1, 0).astype(BF16)
    for i in range(nx):
        xs[i] = dot(dmat[i * rowx:(i + 1) * rowx, :], mine, 1, 0).astype(BF16)
    xr[x] = xs[x]

    pl.semaphore_wait(barrier, len(met))

    def dx_copy(d, slot):
        return copy(xs.at[lax.rem(x + d, nx)], xr.at[slot], dx_s.at[d], dx_r.at[d], at_x(d))

    for d in range(1, nx):
        dx_copy(d, x).start()

    rows_t = ecot.shape[0] // 4
    @pl.loop(0, 4)
    def _(i):
        at = pl.ds(pl.multiple_of(i * rows_t, 16), rows_t)
        prt[at, :] = dot(ecot[at, :], ew[...], 1, 1).astype(BF16)

    blk = nx * CAP
    pz[:, :, :, feat:] = jnp.zeros((2, pairs, blk, fpad - feat), BF16)
    for i in range(2):
        half = p_z[i * pairs * blk:(i + 1) * pairs * blk, :]
        pz[i, :, :, 0:feat] = dot(half, prt[...], 1, 0).astype(BF16).reshape(pairs, blk, feat)

    def pe_copy(k):
        return copy(pz.at[1 - par, k], pin.at[k], pe_s.at[k], pe_r.at[k], beside)

    @pl.loop(0, pairs)
    def _(k):
        pe_copy(k).start()

    def wx_copy(d):
        return copy(wxs.at[d - 1], wxr.at[d - 1], wx_s.at[d], wx_r.at[d], at_x(d))

    def wblock(xx):
        w_in = li[:, pl.ds(pl.multiple_of(xx * win_w, 128), win_w)]
        return dot(cot[...], w_in, 1, 0)

    for d in range(1, nx):
        got = wblock(lax.rem(x + d, nx))
        for q in range(nz):
            wxs[d - 1, rev_bits(q, bits), :, 0:wl] = got[:, q * wl:(q + 1) * wl].astype(BF16)
        wxs[d - 1, :, :, wl:] = jnp.zeros((nz, wxs.shape[2], wxs.shape[3] - wl), BF16)
        wx_copy(d).start()
    got = wblock(x)
    for q in range(nz):
        wz[rev_bits(q, bits), :, 0:wl] = got[:, q * wl:(q + 1) * wl]
    wz[:, :, wl:] = jnp.zeros((nz, wz.shape[1], wz.shape[2] - wl), F32)

    for d in range(1, nx):
        dx_copy(d, lax.rem(x + nx - d, nx)).wait_recv()
    zs[...] = dot(p_x[...], xr[...].reshape(nx * rowx, fpad), 1, 0).astype(BF16).reshape(
        pairs, blk, fpad
    )

    def dz_copy(d, slot):
        return copy(
            zs.at[lax.rem(pair + d, pairs)], zr.at[par, slot], dz_s.at[d], dz_r.at[d], at_pair(d)
        )

    def df_copy(d, side):
        slot = lax.rem(pair + pairs - d, pairs)
        return copy(zr.at[side, slot], zr.at[side, slot], df_s.at[d], df_r.at[d], beside)

    @pl.loop(1, pairs)
    def _(d):
        dz_copy(d, pair).start()

    zr[par, pair] = zs[pair]
    df_copy(0, par).start()

    def rz_copy(d, slot):
        return copy(
            rs.at[lax.rem(pair + d, pairs)], rz.at[slot], rz_s.at[d], rz_r.at[d], at_pair(d)
        )

    @pl.loop(1, pairs)
    def _(d):
        k = lax.rem(pair + d, pairs)
        pe_copy(k).wait_recv()
        rs[k] = (pz[par, k].astype(F32) + pin[k].astype(F32)).astype(BF16)
        rz_copy(d, pair).start()

    pe_copy(pair).wait_recv()
    rz[pair] = (pz[par, pair].astype(F32) + pin[pair].astype(F32)).astype(BF16)

    def c_copy(k):
        return copy(dsend.at[k], dcore.at[k], c_s.at[k], c_r.at[k], other_core)

    @pl.loop(0, nh * ny)
    def _(k):
        part = dot(wt[:, pl.ds(pl.multiple_of(k * chip_w, 128), chip_w)], cot[...], 0, 0)
        low, high = part[0:feat, :], part[feat:, :]
        dacc[k] = jnp.where(core == 0, low, high)
        dsend[k] = jnp.where(core == 0, high, low).astype(BF16)
        c_copy(k).start()

    def y_copy(d):
        return copy(ysend.at[d - 1], yrecv.at[d - 1], y_s.at[d], y_r.at[d], at_y(d))

    def core_sum(k):
        c_copy(k).wait_recv()
        return dacc[k] + dcore[k].astype(F32)

    for d in range(1, ny):
        for h in range(nh):
            ysend[d - 1, h] = core_sum(h * ny + lax.rem(y + d, ny)).astype(BF16)
        y_copy(d).start()
    for h in range(nh):
        dacc[h * ny + y] = core_sum(h * ny + y)

    for d in range(1, nx):
        wx_copy(d).wait_recv()

    @pl.loop(0, nz)
    def _(i):
        total = wz[i]
        for d in range(1, nx):
            total = total + wxr[d - 1, i].astype(F32)
        wz[i] = total

    def wz_at(step):
        base, size = 0, nz
        for b in range(step):
            size = size // 2
            base = base + ((z // (1 << b)) % 2) * size
        return base, size

    def wz_copy(step):
        base, size = wz_at(step)
        size = size // 2
        bit = (z // (1 << step)) % 2
        away = base + (1 - bit) * size
        land = nz - 2 * size
        partner = at_z(z + (1 - 2 * bit) * (1 << step))
        return copy(
            wz.at[pl.ds(away, size)], wzr.at[pl.ds(land, size)],
            wz_s.at[step], wz_r.at[step], partner,
        )

    def wz_add(step):
        wz_copy(step).wait_recv()
        base, size = wz_at(step + 1)
        land = nz - 2 * size

        @pl.loop(0, size)
        def _(i):
            wz[base + i] = wz[base + i] + wzr[land + i]

    wz_copy(0).start()

    @pl.loop(1, pairs)
    def _(d):
        dz_copy(d, lax.rem(pair + pairs - d, pairs)).wait_recv()
        df_copy(d, par).start()

    def h_copy():
        return copy(hsend, hrecv, h_s.at[0], h_r.at[0], other_h)

    for d in range(1, ny):
        y_copy(d).wait_recv()
    for h in range(nh):
        total = dacc[h * ny + y]
        for d in range(1, ny):
            total = total + yrecv[d - 1, h].astype(F32)
        dacc[h * ny + y] = total
    hsend[...] = dacc[(1 - zh) * ny + y].astype(BF16)
    h_copy().start()

    wz_add(0)
    wz_copy(1).start()

    @pl.loop(1, pairs)
    def _(d):
        rz_copy(d, lax.rem(pair + pairs - d, pairs)).wait_recv()

    qs[...] = dot(p_x[...], rz[...].reshape(pairs * blk, fpad), 0, 0).astype(BF16).reshape(
        nx, rowx, fpad
    )

    def rx_copy(d, slot):
        return copy(qs.at[lax.rem(x + d, nx)], rx.at[slot], rx_s.at[d], rx_r.at[d], at_x(d))

    for d in range(1, nx):
        rx_copy(d, x).start()
    rx[x] = qs[x]

    wz_add(1)
    if bits > 2:
        wz_copy(2).start()

    @pl.loop(0, pairs)
    def _(d):
        df_copy(d, 1 - par).wait_recv()

    for i in range(2):
        half = p_z[i * pairs * blk:(i + 1) * pairs * blk, :]
        part = dot(half, zr[i].reshape(pairs * blk, fpad)[:, 0:feat], 0, 0)
        if i == 0:
            ordered = part
        else:
            ordered = ordered + part
    prt[...] = ordered.astype(BF16)
    cols = 256

    @pl.loop(0, ecot.shape[1] // cols)
    def _(i):
        at = pl.ds(pl.multiple_of(i * cols, 128), cols)
        o_ew[:, at] = dot(prt[...], ecot[:, at], 0, 0).astype(BF16)

    for step in range(2, bits):
        wz_add(step)
        if step + 1 < bits:
            wz_copy(step + 1).start()
    base, _ = wz_at(bits)
    o_dw[...] = wz[base][:, 0:wl]

    h_copy().wait_recv()
    for d in range(1, nx):
        rx_copy(d, lax.rem(x + nx - d, nx)).wait_recv()
    expert_sum = dot(rx[...].reshape(nx * rowx, fpad), dmat[...], 0, 0)[0:feat, :]
    dense_sum = dacc[zh * ny + y] + hrecv[...].astype(F32)
    o_in[...] = (expert_sum + dense_sum).astype(BF16)

    for d in range(1, nx):
        dx_copy(d, x).wait_send()
        rx_copy(d, x).wait_send()
        wx_copy(d).wait_send()
    for d in range(1, ny):
        y_copy(d).wait_send()
    h_copy().wait_send()
    for step in range(bits):
        wz_copy(step).wait_send()

    @pl.loop(1, pairs)
    def _(d):
        dz_copy(d, pair).wait_send()
        rz_copy(d, pair).wait_send()

    @pl.loop(0, pairs)
    def _(d):
        df_copy(d, par).wait_send()
        pe_copy(d).wait_send()

    @pl.loop(0, nh * ny)
    def _(k):
        c_copy(k).wait_send()


def body(nx, ny, layer_input, routes, dense_cot, dense_weight, expert_cot, expert_weight):
    nz = lax.axis_size("expert") // nx
    nh = lax.axis_size("dp") // ny
    pairs = nz // 2
    bits = nz.bit_length() - 1
    experts = nx * pairs
    tok, width = layer_input.shape
    feat, cols = expert_weight.shape
    hid = dense_cot.shape[1]
    slots = experts * CAP
    rows = 2 * slots
    fpad = up(feat, 128)
    wl = width // (nx * nz)
    wpad = up(wl, 128)
    rowx, blk = pairs * CAP, nx * CAP

    px = np.zeros((slots, slots), np.float32)
    for p in range(pairs):
        for s in range(nx):
            for c in range(CAP):
                px[p * blk + s * CAP + c, s * rowx + p * CAP + c] = 1
    pz = np.zeros((rows, rows), np.float32)
    for q in range(nz):
        for s in range(nx):
            for c in range(CAP):
                pz[(q % 2) * slots + (q // 2) * blk + s * CAP + c, (s * nz + q) * CAP + c] = 1
    slot = np.arange(slots)
    e_mat = (slot[:, None] // CAP == np.arange(experts)[None, :]).astype(np.float32)
    m_mat = np.broadcast_to((slot % CAP)[:, None], (slots, tok)).astype(np.float32)

    dma = pltpu.SemaphoreType.DMA
    vm = pltpu.VMEM
    groups = nh * ny
    scratch = [
        vm((slots, tok), BF16),
        vm((nx, rowx, fpad), BF16), vm((nx, rowx, fpad), BF16),
        vm((pairs, blk, fpad), BF16), vm((2, pairs, blk, fpad), BF16),
        vm((rows, feat), BF16), vm((2, pairs, blk, fpad), BF16), vm((pairs, blk, fpad), BF16),
        vm((pairs, blk, fpad), BF16), vm((pairs, blk, fpad), BF16),
        vm((nx, rowx, fpad), BF16), vm((nx, rowx, fpad), BF16),
        vm((groups, feat, tok), F32), vm((groups, feat, tok), BF16), vm((groups, feat, tok), BF16),
        vm((ny - 1, nh, feat, tok), BF16), vm((ny - 1, nh, feat, tok), BF16),
        vm((feat, tok), BF16), vm((feat, tok), BF16),
        vm((nx - 1, nz, hid, wpad), BF16), vm((nx - 1, nz, hid, wpad), BF16),
        vm((nz, hid, wpad), F32), vm((nz, hid, wpad), F32),
    ]
    for count in (nx, pairs, pairs, pairs, pairs, nx, groups, ny, 1, nx, bits):
        scratch += [dma((count,)), dma((count,))]
    full = pl.BlockSpec(memory_space=pltpu.VMEM)
    in_t, dw_t, ew_out = pl.pallas_call(
        functools.partial(kernel, (nx, nz, ny, nh)),
        out_shape=(
            jax.ShapeDtypeStruct((feat, tok), BF16),
            jax.ShapeDtypeStruct((hid, wl), F32),
            jax.ShapeDtypeStruct((feat, cols), BF16),
        ),
        in_specs=[full] * 10,
        out_specs=(full, full, full),
        scratch_shapes=scratch,
        compiler_params=pltpu.CompilerParams(
            collective_id=0, has_side_effects=True, vmem_limit_bytes=56 * 1024 * 1024
        ),
    )(
        layer_input, routes.T, dense_cot.T, dense_weight.T, expert_cot, expert_weight,
        jnp.asarray(px, BF16), jnp.asarray(pz, BF16), jnp.asarray(e_mat, BF16),
        jnp.asarray(m_mat, F32),
    )
    return (in_t.T, dw_t.T, ew_out)


def solution(mesh, nx=NX, ny=NY):
    placed = (
        P("expert", None),
        P("expert", None),
        P("expert", ("dp", "tensor")),
        P(None, ("dp", "tensor")),
        P(None, "expert"),
        P(("dp", "tensor"), "expert"),
    )
    return jax.shard_map(
        functools.partial(body, nx, ny),
        mesh=mesh,
        in_specs=placed,
        out_specs=(
            P("expert", ("dp", "tensor")),
            P("expert", ("dp", "tensor")),
            P(("dp", "tensor"), "expert"),
        ),
        check_vma=False,
    )
```

time: 1080 us -> 194 us (0.18)
  the two profiles are of different devices: /device:TPU:24 before, /device:TPU:214 now
where the time goes in v1:
time: 194 us
  Pallas kernels  188 us (97%)
  local copies, waits for them, and re-layouts  5.41 us (3%)
    pallas_call x1, Pallas kernels, body(): pl.pallas_call(functools.partial(kernel, (nx, nz, ny, nh)), out_shape=(ja...  188 us
    unnamed x3, local copies, waits for them, and re-layouts  5.41 us

profile of v1, /device:TPU:214, one launch (start us, length us, event | category | flops | bytes accessed | tf_op | source)
XLA Modules:
  0.0 194.2 jit_solution(12063250513274743862)
XLA Ops:
  0.6 188.2 %shard_map.121 = (bf16[448,128]{1,0:T(8,128)(2,1)}, f32[160,112]{1,0:T(8,128)}, bf16[448,1280]{1,0:T(8,128)(2,1)}) custom-call(bf16[128,7168]{1,0:T(8,128)(2,1)} %li.1, s32[2,128]{1,0:T(2,128)} %bitcast.9, bf16[160,128]{1,0:T(8,128)(2,1)} %bitcast.8, bf16[160,7168]{1,0:T(8,128)(2,1)} %bitcast.5, bf16[768,1280]{1,0:T(8,128)(2,1)} %ecot.1, ...), custom_call_target="tpu_custom_call" | custom-call | tf_op jit(solution)/shard_map/pallas_call | solution.py:399
  188.8 1.6 copy.16
  190.4 1.5 copy.17
  191.9 2.3 %copy.18 = bf16[448,1280]{1,0:T(8,128)(2,1)} copy(bf16[448,1280]{1,0:T(8,128)(2,1)} %get-tuple-element.14) | data formatting | bytes 2293760

commit v2 on v1

--- a/solution.py
+++ b/solution.py
@@ -33,7 +33,7 @@
     o_in, o_dw, o_ew,
     dmat, xs, xr, zs, zr, prt, pz, pin, rs, rz, qs, rx,
     dacc, dsend, dcore, ysend, yrecv, hsend, hrecv,
-    wxs, wxr, wz, wzr,
+    wxs, wxr, wz, wzs, wzr, in_sem,
     dx_s, dx_r, dz_s, dz_r, df_s, df_r, pe_s, pe_r, rz_s, rz_r, rx_s, rx_r,
     c_s, c_r, y_s, y_r, h_s, h_r, wx_s, wx_r, wz_s, wz_r,
 ):
@@ -75,11 +75,54 @@
             device_id=dev, device_id_type=MESH,
         )
 
-    met = [at_x(d) for d in range(1, nx)] + [at_pair(d) for d in range(1, pairs)]
-    met += [beside, other_core] + [at_y(d) for d in range(1, ny)] + [other_h]
+    blk = nx * CAP
+    higher_z, higher_beside, higher_h = in_sem.at[1], in_sem.at[0], in_sem.at[2]
+
+    def signal(sem, dev):
+        pl.semaphore_signal(sem, inc=1, device_id=dev, device_id_type=MESH)
+
+    def at_ring(d):
+        around = zh * pairs + pair + d - pairs * ((2 * d + core) // (pairs + 1))
+        around = lax.rem(around + nh * pairs, nh * pairs)
+        return ((around // pairs) * ny + y, x * nz + lax.rem(around, pairs) * 2 + par, core)
+
+    def at_other_h(k):
+        return ((1 - zh) * ny + y, x * nz + k * 2 + par, core)
+
+    same_z = [at_x(d) for d in range(1, nx)] + [other_core] + [at_y(d) for d in range(1, ny)]
     barrier = pltpu.get_barrier_semaphore()
-    for dev in met:
-        pl.semaphore_signal(barrier, inc=1, device_id=dev, device_id_type=MESH)
+    for dev in same_z:
+        signal(barrier, dev)
+
+    @pl.when(par == 0)
+    def _():
+        signal(barrier, beside)
+
+    @pl.loop(0, pairs)
+    def _(k):
+        @pl.when(k > pair)
+        def _():
+            signal(barrier, at_z(2 * k + par))
+
+        @pl.when(zh == 0)
+        def _():
+            signal(barrier, at_other_h(k))
+
+    pl.semaphore_wait(barrier, len(same_z) + pair + par + zh * pairs)
+
+    @pl.when(par == 1)
+    def _():
+        signal(higher_beside, beside)
+
+    @pl.loop(0, pairs)
+    def _(k):
+        @pl.when(k < pair)
+        def _():
+            signal(higher_z, at_z(2 * k + par))
+
+        @pl.when(zh == 1)
+        def _():
+            signal(higher_h, at_other_h(k))
 
     r = rt[...]
     e_row = lax.broadcasted_iota(jnp.int32, (e_mat.shape[1], r.shape[1]), 0)
@@ -93,16 +136,24 @@
     ranks = dot(e_mat[...], rank, 1, 0)
     dmat[...] = ((is_member > 0.5) & (ranks == m_mat[...])).astype(F32).astype(BF16)
     chip_w = 2 * feat
-    window = li[:, pl.ds(pl.multiple_of(dp * chip_w, 128), chip_w)]
     pick_r = lax.broadcasted_iota(jnp.int32, (chip_w, fpad), 0)
     pick_c = lax.broadcasted_iota(jnp.int32, (chip_w, fpad), 1)
     pick = ((pick_r == pick_c + core * feat) & (pick_c < feat)).astype(F32).astype(BF16)
-    mine = dot(window, pick, 1, 0).astype(BF16)
+
+    def features(group):
+        window = li[:, pl.ds(pl.multiple_of(group * chip_w, 128), chip_w)]
+        return dot(window, pick, 1, 0).astype(BF16)
+
+    mine, theirs = features(dp), features((1 - zh) * ny + y)
+    row = lax.broadcasted_iota(jnp.int32, (rowx, fpad), 0)
+    to_pair = sum((row >= k * CAP).astype(jnp.int32) for k in range(1, pairs))
+    dist = to_pair - pair + jnp.where(to_pair < pair, pairs, 0)
+    back = (dist > pairs // 2) | ((dist == pairs // 2) & (core == 1))
+    crosses = pair + dist - jnp.where(back, pairs, 0) != to_pair
     for i in range(nx):
-        xs[i] = dot(dmat[i * rowx:(i + 1) * rowx, :], mine, 1, 0).astype(BF16)
+        rows_i = dmat[i * rowx:(i + 1) * rowx, :]
+        xs[i] = jnp.where(crosses, dot(rows_i, theirs, 1, 0), dot(rows_i, mine, 1, 0)).astype(BF16)
     xr[x] = xs[x]
-
-    pl.semaphore_wait(barrier, len(met))
 
     def dx_copy(d, slot):
         return copy(xs.at[lax.rem(x + d, nx)], xr.at[slot], dx_s.at[d], dx_r.at[d], at_x(d))
@@ -116,7 +167,6 @@
         at = pl.ds(pl.multiple_of(i * rows_t, 16), rows_t)
         prt[at, :] = dot(ecot[at, :], ew[...], 1, 1).astype(BF16)
 
-    blk = nx * CAP
     pz[:, :, :, feat:] = jnp.zeros((2, pairs, blk, fpad - feat), BF16)
     for i in range(2):
         half = p_z[i * pairs * blk:(i + 1) * pairs * blk, :]
@@ -125,9 +175,24 @@
     def pe_copy(k):
         return copy(pz.at[1 - par, k], pin.at[k], pe_s.at[k], pe_r.at[k], beside)
 
+    @pl.when(par == 0)
+    def _():
+        pl.semaphore_wait(higher_beside, 1)
+
     @pl.loop(0, pairs)
     def _(k):
         pe_copy(k).start()
+
+    def c_copy(k):
+        return copy(dsend.at[k], dcore.at[k], c_s.at[k], c_r.at[k], other_core)
+
+    @pl.loop(0, nh * ny)
+    def _(k):
+        part = dot(wt[:, pl.ds(pl.multiple_of(k * chip_w, 128), chip_w)], cot[...], 0, 0)
+        low, high = part[0:feat, :], part[feat:, :]
+        dacc[k] = jnp.where(core == 0, low, high)
+        dsend[k] = jnp.where(core == 0, high, low).astype(BF16)
+        c_copy(k).start()
 
     def wx_copy(d):
         return copy(wxs.at[d - 1], wxr.at[d - 1], wx_s.at[d], wx_r.at[d], at_x(d))
@@ -147,54 +212,6 @@
         wz[rev_bits(q, bits), :, 0:wl] = got[:, q * wl:(q + 1) * wl]
     wz[:, :, wl:] = jnp.zeros((nz, wz.shape[1], wz.shape[2] - wl), F32)
 
-    for d in range(1, nx):
-        dx_copy(d, lax.rem(x + nx - d, nx)).wait_recv()
-    zs[...] = dot(p_x[...], xr[...].reshape(nx * rowx, fpad), 1, 0).astype(BF16).reshape(
-        pairs, blk, fpad
-    )
-
-    def dz_copy(d, slot):
-        return copy(
-            zs.at[lax.rem(pair + d, pairs)], zr.at[par, slot], dz_s.at[d], dz_r.at[d], at_pair(d)
-        )
-
-    def df_copy(d, side):
-        slot = lax.rem(pair + pairs - d, pairs)
-        return copy(zr.at[side, slot], zr.at[side, slot], df_s.at[d], df_r.at[d], beside)
-
-    @pl.loop(1, pairs)
-    def _(d):
-        dz_copy(d, pair).start()
-
-    zr[par, pair] = zs[pair]
-    df_copy(0, par).start()
-
-    def rz_copy(d, slot):
-        return copy(
-            rs.at[lax.rem(pair + d, pairs)], rz.at[slot], rz_s.at[d], rz_r.at[d], at_pair(d)
-        )
-
-    @pl.loop(1, pairs)
-    def _(d):
-        k = lax.rem(pair + d, pairs)
-        pe_copy(k).wait_recv()
-        rs[k] = (pz[par, k].astype(F32) + pin[k].astype(F32)).astype(BF16)
-        rz_copy(d, pair).start()
-
-    pe_copy(pair).wait_recv()
-    rz[pair] = (pz[par, pair].astype(F32) + pin[pair].astype(F32)).astype(BF16)
-
-    def c_copy(k):
-        return copy(dsend.at[k], dcore.at[k], c_s.at[k], c_r.at[k], other_core)
-
-    @pl.loop(0, nh * ny)
-    def _(k):
-        part = dot(wt[:, pl.ds(pl.multiple_of(k * chip_w, 128), chip_w)], cot[...], 0, 0)
-        low, high = part[0:feat, :], part[feat:, :]
-        dacc[k] = jnp.where(core == 0, low, high)
-        dsend[k] = jnp.where(core == 0, high, low).astype(BF16)
-        c_copy(k).start()
-
     def y_copy(d):
         return copy(ysend.at[d - 1], yrecv.at[d - 1], y_s.at[d], y_r.at[d], at_y(d))
 
@@ -210,14 +227,47 @@
         dacc[h * ny + y] = core_sum(h * ny + y)
 
     for d in range(1, nx):
-        wx_copy(d).wait_recv()
-
-    @pl.loop(0, nz)
-    def _(i):
-        total = wz[i]
-        for d in range(1, nx):
-            total = total + wxr[d - 1, i].astype(F32)
-        wz[i] = total
+        dx_copy(d, lax.rem(x + nx - d, nx)).wait_recv()
+    zs[...] = dot(p_x[...], xr[...].reshape(nx * rowx, fpad), 1, 0).astype(BF16).reshape(
+        pairs, blk, fpad
+    )
+
+    def dz_copy(d, slot):
+        return copy(
+            zs.at[lax.rem(pair + d, pairs)], zr.at[par, slot], dz_s.at[d], dz_r.at[d], at_ring(d)
+        )
+
+    def df_copy(d, side):
+        slot = lax.rem(pair + pairs - d, pairs)
+        return copy(zr.at[side, slot], zr.at[side, slot], df_s.at[d], df_r.at[d], beside)
+
+    zr[par, pair] = zs[pair]
+    df_copy(0, par).start()
+
+    @pl.when(pair < pairs - 1)
+    def _():
+        pl.semaphore_wait(higher_z, pairs - 1 - pair)
+
+    def rz_copy(d, slot):
+        return copy(
+            rs.at[lax.rem(pair + d, pairs)], rz.at[slot], rz_s.at[d], rz_r.at[d], at_pair(d)
+        )
+
+    @pl.loop(1, pairs)
+    def _(d):
+        k = lax.rem(pair + d, pairs)
+        pe_copy(k).wait_recv()
+        rs[k] = (pz[par, k].astype(F32) + pin[k].astype(F32)).astype(BF16)
+        rz_copy(d, pair).start()
+
+    pe_copy(pair).wait_recv()
+    rz[pair] = (pz[par, pair].astype(F32) + pin[pair].astype(F32)).astype(BF16)
+
+    @pl.loop(1, pairs)
+    def _(d):
+        @pl.when(at_ring(d)[0] == dp)
+        def _():
+            dz_copy(d, pair).start()
 
     def wz_at(step):
         base, size = 0, nz
@@ -227,32 +277,45 @@
         return base, size
 
     def wz_copy(step):
+        size = nz >> (step + 1)
+        at = pl.ds(nz - 2 * size, size)
+        bit = (z // (1 << step)) % 2
+        partner = at_z(z + (1 - 2 * bit) * (1 << step))
+        return copy(wzs.at[at], wzr.at[at], wz_s.at[step], wz_r.at[step], partner)
+
+    def wz_step(step, total):
         base, size = wz_at(step)
-        size = size // 2
-        bit = (z // (1 << step)) % 2
-        away = base + (1 - bit) * size
-        land = nz - 2 * size
-        partner = at_z(z + (1 - 2 * bit) * (1 << step))
-        return copy(
-            wz.at[pl.ds(away, size)], wzr.at[pl.ds(land, size)],
-            wz_s.at[step], wz_r.at[step], partner,
-        )
-
-    def wz_add(step):
-        wz_copy(step).wait_recv()
-        base, size = wz_at(step + 1)
-        land = nz - 2 * size
+        if step < bits:
+            size = size // 2
+            bit = (z // (1 << step)) % 2
+            away, base = base + (1 - bit) * size, base + bit * size
+
+            @pl.loop(0, size)
+            def _(i):
+                wzs[nz - 2 * size + i] = total(away + i).astype(BF16)
+
+            wz_copy(step).start()
 
         @pl.loop(0, size)
         def _(i):
-            wz[base + i] = wz[base + i] + wzr[land + i]
-
-    wz_copy(0).start()
-
-    @pl.loop(1, pairs)
-    def _(d):
-        dz_copy(d, lax.rem(pair + pairs - d, pairs)).wait_recv()
-        df_copy(d, par).start()
+            wz[base + i] = total(base + i)
+
+    def wz_next(step):
+        wz_copy(step - 1).wait_recv()
+        base, size = wz_at(step)
+        land = nz - 2 * size
+        wz_step(step, lambda i: wz[i] + wzr[land + i - base].astype(F32))
+
+    for d in range(1, nx):
+        wx_copy(d).wait_recv()
+
+    def over_x(i):
+        total = wz[i]
+        for d in range(1, nx):
+            total = total + wxr[d - 1, i].astype(F32)
+        return total
+
+    wz_step(0, over_x)
 
     def h_copy():
         return copy(hsend, hrecv, h_s.at[0], h_r.at[0], other_h)
@@ -265,10 +328,25 @@
             total = total + yrecv[d - 1, h].astype(F32)
         dacc[h * ny + y] = total
     hsend[...] = dacc[(1 - zh) * ny + y].astype(BF16)
+
+    @pl.when(zh == 0)
+    def _():
+        pl.semaphore_wait(higher_h, pairs)
+
+    @pl.loop(1, pairs)
+    def _(d):
+        @pl.when(at_ring(d)[0] != dp)
+        def _():
+            dz_copy(d, pair).start()
+
     h_copy().start()
 
-    wz_add(0)
-    wz_copy(1).start()
+    @pl.loop(1, pairs)
+    def _(d):
+        dz_copy(d, lax.rem(pair + pairs - d, pairs)).wait_recv()
+        df_copy(d, par).start()
+
+    wz_next(1)
 
     @pl.loop(1, pairs)
     def _(d):
@@ -285,9 +363,8 @@
         rx_copy(d, x).start()
     rx[x] = qs[x]
 
-    wz_add(1)
     if bits > 2:
-        wz_copy(2).start()
+        wz_next(2)
 
     @pl.loop(0, pairs)
     def _(d):
@@ -308,10 +385,8 @@
         at = pl.ds(pl.multiple_of(i * cols, 128), cols)
         o_ew[:, at] = dot(prt[...], ecot[:, at], 0, 0).astype(BF16)
 
-    for step in range(2, bits):
-        wz_add(step)
-        if step + 1 < bits:
-            wz_copy(step + 1).start()
+    for step in range(min(3, bits), bits + 1):
+        wz_next(step)
     base, _ = wz_at(bits)
     o_dw[...] = wz[base][:, 0:wl]
 
@@ -391,7 +466,8 @@
         vm((ny - 1, nh, feat, tok), BF16), vm((ny - 1, nh, feat, tok), BF16),
         vm((feat, tok), BF16), vm((feat, tok), BF16),
         vm((nx - 1, nz, hid, wpad), BF16), vm((nx - 1, nz, hid, wpad), BF16),
-        vm((nz, hid, wpad), F32), vm((nz, hid, wpad), F32),
+        vm((nz, hid, wpad), F32), vm((nz, hid, wpad), BF16), vm((nz, hid, wpad), BF16),
+        pltpu.SemaphoreType.REGULAR((3,)),
     ]
     for count in (nx, pairs, pairs, pairs, pairs, nx, groups, ny, 1, nx, bits):
         scratch += [dma((count,)), dma((count,))]

time: 194 us -> 146 us (0.75)
  the two profiles are of different devices: /device:TPU:214 before, /device:TPU:69 now
where the time goes in v2:
time: 146 us
  Pallas kernels  140 us (96%)
  local copies, waits for them, and re-layouts  5.41 us (4%)
    pallas_call x1, Pallas kernels, body(): pl.pallas_call(functools.partial(kernel, (nx, nz, ny, nh)), out_shape=(ja...  140 us
    unnamed x3, local copies, waits for them, and re-layouts  5.41 us

profile of v2, /device:TPU:69, one launch (start us, length us, event | category | flops | bytes accessed | tf_op | source)
XLA Modules:
  0.0 146.2 jit_solution(4575500834833468148)
XLA Ops:
  0.6 140.1 %shard_map.121 = (bf16[448,128]{1,0:T(8,128)(2,1)}, f32[160,112]{1,0:T(8,128)}, bf16[448,1280]{1,0:T(8,128)(2,1)}) custom-call(bf16[128,7168]{1,0:T(8,128)(2,1)} %li.1, s32[2,128]{1,0:T(2,128)} %bitcast.9, bf16[160,128]{1,0:T(8,128)(2,1)} %bitcast.8, bf16[160,7168]{1,0:T(8,128)(2,1)} %bitcast.5, bf16[768,1280]{1,0:T(8,128)(2,1)} %ecot.1, ...), custom_call_target="tpu_custom_call" | custom-call | tf_op jit(solution)/shard_map/pallas_call | solution.py:475
  140.8 1.6 %copy.16 = bf16[128,448]{0,1:T(8,128)(2,1)} copy(bf16[128,448]{0,1:T(8,128)(2,1)} %bitcast.6) | data formatting | bytes 229376
  142.3 1.5 %copy.17 = f32[112,160]{0,1:T(8,128)} copy(f32[112,160]{0,1:T(8,128)} %bitcast.7) | data formatting | bytes 143360
  143.8 2.3 %copy.18 = bf16[448,1280]{1,0:T(8,128)(2,1)} copy(bf16[448,1280]{1,0:T(8,128)(2,1)} %get-tuple-element.14) | data formatting | bytes 2293760

commit v3 on v2

--- a/solution.py
+++ b/solution.py
@@ -29,15 +29,19 @@
 
 def kernel(
     dims,
-    li, rt, cot, wt, ecot, ew, p_x, p_z, e_mat, m_mat,
+    li, rt, cot, wt_hbm, ecot_hbm, ew_hbm, p_x, p_z_hbm, e_mat, m_mat,
     o_in, o_dw, o_ew,
     dmat, xs, xr, zs, zr, prt, pz, pin, rs, rz, qs, rx,
     dacc, dsend, dcore, ysend, yrecv, hsend, hrecv,
-    wxs, wxr, wz, wzs, wzr, in_sem,
+    wxs, wxr, wz, wzs, wzr, in_sem, wt, ecot, ew, p_z, load_s,
     dx_s, dx_r, dz_s, dz_r, df_s, df_r, pe_s, pe_r, rz_s, rz_r, rx_s, rx_r,
     c_s, c_r, y_s, y_r, h_s, h_r, wx_s, wx_r, wz_s, wz_r,
 ):
     nx, nz, ny, nh = dims
+    from_hbm = ((ecot_hbm, ecot), (ew_hbm, ew), (p_z_hbm, p_z), (wt_hbm, wt))
+    loads = [pltpu.make_async_copy(a, b, load_s.at[i]) for i, (a, b) in enumerate(from_hbm)]
+    for load in loads:
+        load.start()
     pairs = nz // 2
     bits = nz.bit_length() - 1
     feat = ew.shape[0]
@@ -58,9 +62,6 @@
     def at_z(zz):
         return (dp, x * nz + zz, core)
 
-    def at_pair(d):
-        return at_z(lax.rem(pair + d, pairs) * 2 + par)
-
     beside = at_z(z + 1 - 2 * par)
     other_core = (dp, ex, 1 - core)
 
@@ -82,12 +83,19 @@
         pl.semaphore_signal(sem, inc=1, device_id=dev, device_id_type=MESH)
 
     def at_ring(d):
-        around = zh * pairs + pair + d - pairs * ((2 * d + core) // (pairs + 1))
+        around = zh * pairs + pair + d - pairs * goes_back(d)
         around = lax.rem(around + nh * pairs, nh * pairs)
-        return ((around // pairs) * ny + y, x * nz + lax.rem(around, pairs) * 2 + par, core)
-
-    def at_other_h(k):
-        return ((1 - zh) * ny + y, x * nz + k * 2 + par, core)
+        first = lax.rem(around, pairs) * 2 + goes_back(d)
+        return ((around // pairs) * ny + y, x * nz + first, core)
+
+    def goes_back(d):
+        return (2 * d + core) // (pairs + 1)
+
+    def far_first(i):
+        return pairs // 2 + (i // 2) * (1 - 2 * (i % 2))
+
+    def at_other_h(zz):
+        return ((1 - zh) * ny + y, x * nz + zz, core)
 
     same_z = [at_x(d) for d in range(1, nx)] + [other_core] + [at_y(d) for d in range(1, ny)]
     barrier = pltpu.get_barrier_semaphore()
@@ -98,31 +106,31 @@
     def _():
         signal(barrier, beside)
 
-    @pl.loop(0, pairs)
-    def _(k):
-        @pl.when(k > pair)
+    @pl.loop(0, nz)
+    def _(zz):
+        @pl.when(zz // 2 > pair)
         def _():
-            signal(barrier, at_z(2 * k + par))
+            signal(barrier, at_z(zz))
 
         @pl.when(zh == 0)
         def _():
-            signal(barrier, at_other_h(k))
-
-    pl.semaphore_wait(barrier, len(same_z) + pair + par + zh * pairs)
+            signal(barrier, at_other_h(zz))
+
+    pl.semaphore_wait(barrier, len(same_z) + 2 * pair + par + zh * nz)
 
     @pl.when(par == 1)
     def _():
         signal(higher_beside, beside)
 
-    @pl.loop(0, pairs)
-    def _(k):
-        @pl.when(k < pair)
+    @pl.loop(0, nz)
+    def _(zz):
+        @pl.when(zz // 2 < pair)
         def _():
-            signal(higher_z, at_z(2 * k + par))
+            signal(higher_z, at_z(zz))
 
         @pl.when(zh == 1)
         def _():
-            signal(higher_h, at_other_h(k))
+            signal(higher_h, at_other_h(zz))
 
     r = rt[...]
     e_row = lax.broadcasted_iota(jnp.int32, (e_mat.shape[1], r.shape[1]), 0)
@@ -161,6 +169,8 @@
     for d in range(1, nx):
         dx_copy(d, x).start()
 
+    for load in loads[:3]:
+        load.wait()
     rows_t = ecot.shape[0] // 4
     @pl.loop(0, 4)
     def _(i):
@@ -172,16 +182,81 @@
         half = p_z[i * pairs * blk:(i + 1) * pairs * blk, :]
         pz[i, :, :, 0:feat] = dot(half, prt[...], 1, 0).astype(BF16).reshape(pairs, blk, feat)
 
-    def pe_copy(k):
-        return copy(pz.at[1 - par, k], pin.at[k], pe_s.at[k], pe_r.at[k], beside)
+    def pe_copy(sp, k):
+        i = 2 * k + sp
+        return copy(pz.at[sp, k], pin.at[sp, k], pe_s.at[i], pe_r.at[i], beside)
+
+    def on_side(side, k):
+        return (k - pair) * (2 * side - 1) > 0
+
+    def each_on(side, fn):
+        @pl.loop(0, pairs)
+        def _(i):
+            k = i + side * (pairs - 1 - 2 * i)
+
+            @pl.when(on_side(side, k))
+            def _():
+                fn(0, k)
+                fn(1, k)
 
     @pl.when(par == 0)
     def _():
         pl.semaphore_wait(higher_beside, 1)
 
-    @pl.loop(0, pairs)
-    def _(k):
-        pe_copy(k).start()
+    each_on(1 - par, lambda sp, k: pe_copy(sp, k).start())
+    pe_copy(1 - par, pair).start()
+
+    for d in range(1, nx):
+        dx_copy(d, lax.rem(x + nx - d, nx)).wait_recv()
+    zs[...] = dot(p_x[...], xr[...].reshape(nx * rowx, fpad), 1, 0).astype(BF16).reshape(
+        pairs, blk, fpad
+    )
+
+    def dz_copy(d, side, slot):
+        return copy(
+            zs.at[lax.rem(pair + d, pairs)], zr.at[side, slot],
+            dz_s.at[d], dz_r.at[2 * d + side], at_ring(d),
+        )
+
+    def df_copy(d, side):
+        slot = lax.rem(pair + pairs - d, pairs)
+        i = 2 * d + side
+        return copy(zr.at[side, slot], zr.at[side, slot], df_s.at[i], df_r.at[i], beside)
+
+    def each_way(back, fn):
+        @pl.loop(1, pairs)
+        def _(i):
+            d = far_first(i)
+
+            @pl.when(goes_back(d) == back)
+            def _():
+                fn(d, 0)
+                fn(d, 1)
+
+    zr[par, pair] = zs[pair]
+    df_copy(0, par).start()
+
+    def send_rows(same_h):
+        @pl.loop(1, pairs)
+        def _(i):
+            d = far_first(i)
+
+            @pl.when((at_ring(d)[0] == dp) == same_h)
+            def _():
+                dz_copy(d, par, pair).start()
+
+    def wait_higher_z():
+        @pl.when(pair < pairs - 1)
+        def _():
+            pl.semaphore_wait(higher_z, 2 * (pairs - 1 - pair))
+
+    @pl.when(zh == 1)
+    def _():
+        wait_higher_z()
+        send_rows(True)
+        send_rows(False)
+
+    loads[3].wait()
 
     def c_copy(k):
         return copy(dsend.at[k], dcore.at[k], c_s.at[k], c_r.at[k], other_core)
@@ -226,96 +301,29 @@
     for h in range(nh):
         dacc[h * ny + y] = core_sum(h * ny + y)
 
-    for d in range(1, nx):
-        dx_copy(d, lax.rem(x + nx - d, nx)).wait_recv()
-    zs[...] = dot(p_x[...], xr[...].reshape(nx * rowx, fpad), 1, 0).astype(BF16).reshape(
-        pairs, blk, fpad
-    )
-
-    def dz_copy(d, slot):
-        return copy(
-            zs.at[lax.rem(pair + d, pairs)], zr.at[par, slot], dz_s.at[d], dz_r.at[d], at_ring(d)
-        )
-
-    def df_copy(d, side):
-        slot = lax.rem(pair + pairs - d, pairs)
-        return copy(zr.at[side, slot], zr.at[side, slot], df_s.at[d], df_r.at[d], beside)
-
-    zr[par, pair] = zs[pair]
-    df_copy(0, par).start()
-
-    @pl.when(pair < pairs - 1)
+    @pl.when(zh == 0)
     def _():
-        pl.semaphore_wait(higher_z, pairs - 1 - pair)
-
-    def rz_copy(d, slot):
-        return copy(
-            rs.at[lax.rem(pair + d, pairs)], rz.at[slot], rz_s.at[d], rz_r.at[d], at_pair(d)
-        )
-
-    @pl.loop(1, pairs)
-    def _(d):
-        k = lax.rem(pair + d, pairs)
-        pe_copy(k).wait_recv()
-        rs[k] = (pz[par, k].astype(F32) + pin[k].astype(F32)).astype(BF16)
-        rz_copy(d, pair).start()
-
-    pe_copy(pair).wait_recv()
-    rz[pair] = (pz[par, pair].astype(F32) + pin[pair].astype(F32)).astype(BF16)
-
-    @pl.loop(1, pairs)
-    def _(d):
-        @pl.when(at_ring(d)[0] == dp)
-        def _():
-            dz_copy(d, pair).start()
-
-    def wz_at(step):
-        base, size = 0, nz
-        for b in range(step):
-            size = size // 2
-            base = base + ((z // (1 << b)) % 2) * size
-        return base, size
-
-    def wz_copy(step):
-        size = nz >> (step + 1)
-        at = pl.ds(nz - 2 * size, size)
-        bit = (z // (1 << step)) % 2
-        partner = at_z(z + (1 - 2 * bit) * (1 << step))
-        return copy(wzs.at[at], wzr.at[at], wz_s.at[step], wz_r.at[step], partner)
-
-    def wz_step(step, total):
-        base, size = wz_at(step)
-        if step < bits:
-            size = size // 2
-            bit = (z // (1 << step)) % 2
-            away, base = base + (1 - bit) * size, base + bit * size
-
-            @pl.loop(0, size)
-            def _(i):
-                wzs[nz - 2 * size + i] = total(away + i).astype(BF16)
-
-            wz_copy(step).start()
-
-        @pl.loop(0, size)
-        def _(i):
-            wz[base + i] = total(base + i)
-
-    def wz_next(step):
-        wz_copy(step - 1).wait_recv()
-        base, size = wz_at(step)
-        land = nz - 2 * size
-        wz_step(step, lambda i: wz[i] + wzr[land + i - base].astype(F32))
-
-    for d in range(1, nx):
-        wx_copy(d).wait_recv()
-
-    def over_x(i):
-        total = wz[i]
-        for d in range(1, nx):
-            total = total + wxr[d - 1, i].astype(F32)
-        return total
-
-    wz_step(0, over_x)
+        wait_higher_z()
+        send_rows(True)
+
+    def rz_copy(sp, k, slot):
+        return copy(rs.at[sp, k], rz.at[slot], rz_s.at[2 * k + sp], rz_r.at[slot], at_z(2 * k + sp))
+
+    def pair_sum(sp, k):
+        pe_copy(sp, k).wait_recv()
+        return (pz[sp, k].astype(F32) + pin[sp, k].astype(F32)).astype(BF16)
+
+    def return_rows(sp, k):
+        rs[sp, k] = pair_sum(sp, k)
+        rz_copy(sp, k, pair).start()
+
+    each_on(par, return_rows)
+    rz[pair] = pair_sum(par, pair)
+
+    @pl.when(zh == 0)
+    def _():
+        pl.semaphore_wait(higher_h, nz)
+        send_rows(False)
 
     def h_copy():
         return copy(hsend, hrecv, h_s.at[0], h_r.at[0], other_h)
@@ -329,28 +337,69 @@
         dacc[h * ny + y] = total
     hsend[...] = dacc[(1 - zh) * ny + y].astype(BF16)
 
-    @pl.when(zh == 0)
-    def _():
-        pl.semaphore_wait(higher_h, pairs)
-
-    @pl.loop(1, pairs)
-    def _(d):
-        @pl.when(at_ring(d)[0] != dp)
+    h_copy().start()
+
+    def wz_at(step):
+        base, size = 0, nz
+        for b in range(step):
+            size = size // 2
+            base = base + ((z // (1 << b)) % 2) * size
+        return base, size
+
+    def wz_copy(step):
+        size = nz >> (step + 1)
+        at = pl.ds(nz - 2 * size, size)
+        bit = (z // (1 << step)) % 2
+        partner = at_z(z + (1 - 2 * bit) * (1 << step))
+        return copy(wzs.at[at], wzr.at[at], wz_s.at[step], wz_r.at[step], partner)
+
+    def wz_step(step, total):
+        base, size = wz_at(step)
+        if step < bits:
+            size = size // 2
+            bit = (z // (1 << step)) % 2
+            away, base = base + (1 - bit) * size, base + bit * size
+
+            @pl.loop(0, size)
+            def _(i):
+                wzs[nz - 2 * size + i] = total(away + i).astype(BF16)
+
+            wz_copy(step).start()
+
+        @pl.loop(0, size)
+        def _(i):
+            wz[base + i] = total(base + i)
+
+    def wz_next(step):
+        wz_copy(step - 1).wait_recv()
+        base, size = wz_at(step)
+        land = nz - 2 * size
+        wz_step(step, lambda i: wz[i] + wzr[land + i - base].astype(F32))
+
+    for d in range(1, nx):
+        wx_copy(d).wait_recv()
+
+    def over_x(i):
+        total = wz[i]
+        for d in range(1, nx):
+            total = total + wxr[d - 1, i].astype(F32)
+        return total
+
+    wz_step(0, over_x)
+
+    def forward(d, side):
+        dz_copy(d, side, lax.rem(pair + pairs - d, pairs)).wait_recv()
+        df_copy(d, side).start()
+
+    each_way(par, forward)
+
+    wz_next(1)
+
+    @pl.loop(0, pairs)
+    def _(k):
+        @pl.when(k != pair)
         def _():
-            dz_copy(d, pair).start()
-
-    h_copy().start()
-
-    @pl.loop(1, pairs)
-    def _(d):
-        dz_copy(d, lax.rem(pair + pairs - d, pairs)).wait_recv()
-        df_copy(d, par).start()
-
-    wz_next(1)
-
-    @pl.loop(1, pairs)
-    def _(d):
-        rz_copy(d, lax.rem(pair + pairs - d, pairs)).wait_recv()
+            rz_copy(par, k, k).wait_recv()
 
     qs[...] = dot(p_x[...], rz[...].reshape(pairs * blk, fpad), 0, 0).astype(BF16).reshape(
         nx, rowx, fpad
@@ -366,9 +415,8 @@
     if bits > 2:
         wz_next(2)
 
-    @pl.loop(0, pairs)
-    def _(d):
-        df_copy(d, 1 - par).wait_recv()
+    each_way(1 - par, lambda d, side: df_copy(d, side).wait_recv())
+    df_copy(0, 1 - par).wait_recv()
 
     for i in range(2):
         half = p_z[i * pairs * blk:(i + 1) * pairs * blk, :]
@@ -409,13 +457,13 @@
 
     @pl.loop(1, pairs)
     def _(d):
-        dz_copy(d, pair).wait_send()
-        rz_copy(d, pair).wait_send()
-
-    @pl.loop(0, pairs)
-    def _(d):
-        df_copy(d, par).wait_send()
-        pe_copy(d).wait_send()
+        dz_copy(d, par, pair).wait_send()
+
+    each_way(par, lambda d, side: df_copy(d, side).wait_send())
+    df_copy(0, par).wait_send()
+    each_on(1 - par, lambda sp, k: pe_copy(sp, k).wait_send())
+    pe_copy(1 - par, pair).wait_send()
+    each_on(par, lambda sp, k: rz_copy(sp, k, pair).wait_send())
 
     @pl.loop(0, nh * ny)
     def _(k):
@@ -459,8 +507,8 @@
         vm((slots, tok), BF16),
         vm((nx, rowx, fpad), BF16), vm((nx, rowx, fpad), BF16),
         vm((pairs, blk, fpad), BF16), vm((2, pairs, blk, fpad), BF16),
-        vm((rows, feat), BF16), vm((2, pairs, blk, fpad), BF16), vm((pairs, blk, fpad), BF16),
-        vm((pairs, blk, fpad), BF16), vm((pairs, blk, fpad), BF16),
+        vm((rows, feat), BF16), vm((2, pairs, blk, fpad), BF16), vm((2, pairs, blk, fpad), BF16),
+        vm((2, pairs, blk, fpad), BF16), vm((pairs, blk, fpad), BF16),
         vm((nx, rowx, fpad), BF16), vm((nx, rowx, fpad), BF16),
         vm((groups, feat, tok), F32), vm((groups, feat, tok), BF16), vm((groups, feat, tok), BF16),
         vm((ny - 1, nh, feat, tok), BF16), vm((ny - 1, nh, feat, tok), BF16),
@@ -468,10 +516,13 @@
         vm((nx - 1, nz, hid, wpad), BF16), vm((nx - 1, nz, hid, wpad), BF16),
         vm((nz, hid, wpad), F32), vm((nz, hid, wpad), BF16), vm((nz, hid, wpad), BF16),
         pltpu.SemaphoreType.REGULAR((3,)),
+        vm((hid, width), BF16), vm((rows, cols), BF16), vm((feat, cols), BF16),
+        vm((rows, rows), BF16), dma((4,)),
     ]
-    for count in (nx, pairs, pairs, pairs, pairs, nx, groups, ny, 1, nx, bits):
+    for count in (nx, nz, nz, nz, nz, nx, groups, ny, 1, nx, bits):
         scratch += [dma((count,)), dma((count,))]
     full = pl.BlockSpec(memory_space=pltpu.VMEM)
+    hbm = pl.BlockSpec(memory_space=pl.ANY)
     in_t, dw_t, ew_out = pl.pallas_call(
         functools.partial(kernel, (nx, nz, ny, nh)),
         out_shape=(
@@ -479,7 +530,7 @@
             jax.ShapeDtypeStruct((hid, wl), F32),
             jax.ShapeDtypeStruct((feat, cols), BF16),
         ),
-        in_specs=[full] * 10,
+        in_specs=[full] * 3 + [hbm] * 3 + [full, hbm, full, full],
         out_specs=(full, full, full),
         scratch_shapes=scratch,
         compiler_params=pltpu.CompilerParams(

time: 146 us -> 138 us (0.945)
  the two profiles are of different devices: /device:TPU:69 before, /device:TPU:1 now
where the time goes in v3:
time: 138 us; the launch traced here: 137 us
  Pallas kernels  131 us (95%)
  local copies, waits for them, and re-layouts  5.41 us (4%)
    pallas_call x1, Pallas kernels, body(): pl.pallas_call(functools.partial(kernel, (nx, nz, ny, nh)), out_shape=(ja...  131 us
    unnamed x3, local copies, waits for them, and re-layouts  5.41 us

profile of v3, /device:TPU:1, one launch (start us, length us, event | category | flops | bytes accessed | tf_op | source)
XLA Modules:
  0.0 137.3 jit_solution(12497745867921765006)
XLA Ops:
  0.6 131.3 %shard_map.121 = (bf16[448,128]{1,0:T(8,128)(2,1)}, f32[160,112]{1,0:T(8,128)}, bf16[448,1280]{1,0:T(8,128)(2,1)}) custom-call(bf16[128,7168]{1,0:T(8,128)(2,1)} %li.1, s32[2,128]{1,0:T(2,128)} %bitcast.9, bf16[160,128]{1,0:T(8,128)(2,1)} %bitcast.8, bf16[160,7168]{1,0:T(8,128)(2,1)} %bitcast.5, bf16[768,1280]{1,0:T(8,128)(2,1)} %ecot_hbm.1, ...), custom_call_target="tpu_custom_call" | custom-call | tf_op jit(solution)/shard_map/pallas_call | solution.py:526
  131.9 1.6 %copy.16 = bf16[128,448]{0,1:T(8,128)(2,1)} copy(bf16[128,448]{0,1:T(8,128)(2,1)} %bitcast.6) | data formatting | bytes 229376
  133.4 1.5 %copy.17 = f32[112,160]{0,1:T(8,128)} copy(f32[112,160]{0,1:T(8,128)} %bitcast.7) | data formatting | bytes 143360
  135.0 2.3 %copy.18 = bf16[448,1280]{1,0:T(8,128)(2,1)} copy(bf16[448,1280]{1,0:T(8,128)(2,1)} %get-tuple-element.14) | data formatting | bytes 2293760

commit v4 on v3

--- a/solution.py
+++ b/solution.py
@@ -25,6 +25,35 @@
 
 def up(n, m):
     return -(-n // m) * m
+
+
+def pack(v, blk, feat):
+    n = v.shape[0] // blk
+    whole, rest = feat // 128, feat % 128
+    v = v.reshape(n, blk, v.shape[1])
+    parts = [v[:, :, t * 128:(t + 1) * 128] for t in range(whole)]
+    if rest:
+        half = blk // 2
+        last = v[:, :, whole * 128:feat]
+        parts.append(jnp.concatenate([last[:, :half, :], last[:, half:, :]], axis=2))
+        parts.append(jnp.zeros((n, packed_rows(blk, feat) - whole * blk - half, 128), v.dtype))
+    return jnp.concatenate(parts, axis=1)
+
+
+def unpack(v, blk, feat):
+    n = v.shape[0]
+    whole, rest = feat // 128, feat % 128
+    parts = [v[:, t * blk:(t + 1) * blk, :].reshape(n * blk, 128) for t in range(whole)]
+    if rest:
+        half = blk // 2
+        last = v[:, whole * blk:, :].astype(F32)
+        last = jnp.concatenate([last[:, :half, :rest], last[:, :half, rest:]], axis=1)
+        parts.append(last.reshape(n * blk, rest).astype(v.dtype))
+    return jnp.concatenate(parts, axis=1) if len(parts) > 1 else parts[0]
+
+
+def packed_rows(blk, feat):
+    return feat // 128 * blk + (up(blk // 2, 16) if feat % 128 else 0)
 
 
 def kernel(
@@ -177,10 +206,9 @@
         at = pl.ds(pl.multiple_of(i * rows_t, 16), rows_t)
         prt[at, :] = dot(ecot[at, :], ew[...], 1, 1).astype(BF16)
 
-    pz[:, :, :, feat:] = jnp.zeros((2, pairs, blk, fpad - feat), BF16)
     for i in range(2):
         half = p_z[i * pairs * blk:(i + 1) * pairs * blk, :]
-        pz[i, :, :, 0:feat] = dot(half, prt[...], 1, 0).astype(BF16).reshape(pairs, blk, feat)
+        pz[i] = pack(dot(half, prt[...], 1, 0), blk, feat).astype(BF16)
 
     def pe_copy(sp, k):
         i = 2 * k + sp
@@ -208,9 +236,8 @@
 
     for d in range(1, nx):
         dx_copy(d, lax.rem(x + nx - d, nx)).wait_recv()
-    zs[...] = dot(p_x[...], xr[...].reshape(nx * rowx, fpad), 1, 0).astype(BF16).reshape(
-        pairs, blk, fpad
-    )
+    sorted_rows = dot(p_x[...], xr[...].reshape(nx * rowx, fpad), 1, 0)
+    zs[...] = pack(sorted_rows, blk, feat).astype(BF16)
 
     def dz_copy(d, side, slot):
         return copy(
@@ -401,9 +428,9 @@
         def _():
             rz_copy(par, k, k).wait_recv()
 
-    qs[...] = dot(p_x[...], rz[...].reshape(pairs * blk, fpad), 0, 0).astype(BF16).reshape(
-        nx, rowx, fpad
-    )
+    back_rows = dot(p_x[...], unpack(rz[...], blk, feat), 0, 0).astype(BF16)
+    qs[:, :, 0:feat] = back_rows.reshape(nx, rowx, feat)
+    qs[:, :, feat:] = jnp.zeros((nx, rowx, fpad - feat), BF16)
 
     def rx_copy(d, slot):
         return copy(qs.at[lax.rem(x + d, nx)], rx.at[slot], rx_s.at[d], rx_r.at[d], at_x(d))
@@ -420,7 +447,7 @@
 
     for i in range(2):
         half = p_z[i * pairs * blk:(i + 1) * pairs * blk, :]
-        part = dot(half, zr[i].reshape(pairs * blk, fpad)[:, 0:feat], 0, 0)
+        part = dot(half, unpack(zr[i], blk, feat), 0, 0)
         if i == 0:
             ordered = part
         else:
@@ -485,6 +512,7 @@
     wl = width // (nx * nz)
     wpad = up(wl, 128)
     rowx, blk = pairs * CAP, nx * CAP
+    prows = packed_rows(blk, feat)
 
     px = np.zeros((slots, slots), np.float32)
     for p in range(pairs):
@@ -506,9 +534,9 @@
     scratch = [
         vm((slots, tok), BF16),
         vm((nx, rowx, fpad), BF16), vm((nx, rowx, fpad), BF16),
-        vm((pairs, blk, fpad), BF16), vm((2, pairs, blk, fpad), BF16),
-        vm((rows, feat), BF16), vm((2, pairs, blk, fpad), BF16), vm((2, pairs, blk, fpad), BF16),
-        vm((2, pairs, blk, fpad), BF16), vm((pairs, blk, fpad), BF16),
+        vm((pairs, prows, 128), BF16), vm((2, pairs, prows, 128), BF16),
+        vm((rows, feat), BF16), vm((2, pairs, prows, 128), BF16), vm((2, pairs, prows, 128), BF16),
+        vm((2, pairs, prows, 128), BF16), vm((pairs, prows, 128), BF16),
         vm((nx, rowx, fpad), BF16), vm((nx, rowx, fpad), BF16),
         vm((groups, feat, tok), F32), vm((groups, feat, tok), BF16), vm((groups, feat, tok), BF16),
         vm((ny - 1, nh, feat, tok), BF16), vm((ny - 1, nh, feat, tok), BF16),

time: 138 us -> 134 us (0.971)
  the two profiles are of different devices: /device:TPU:1 before, /device:TPU:5 now
where the time goes in v4:
time: 134 us
  Pallas kernels  128 us (96%)
  local copies, waits for them, and re-layouts  5.41 us (4%)
    pallas_call x1, Pallas kernels, body(): pl.pallas_call(functools.partial(kernel, (nx, nz, ny, nh)), out_shape=(ja...  128 us
    unnamed x3, local copies, waits for them, and re-layouts  5.41 us

profile of v4, /device:TPU:5, one launch (start us, length us, event | category | flops | bytes accessed | tf_op | source)
XLA Modules:
  0.0 133.7 jit_solution(7349610436701201503)
XLA Ops:
  0.6 127.7 %shard_map.121 = (bf16[448,128]{1,0:T(8,128)(2,1)}, f32[160,112]{1,0:T(8,128)}, bf16[448,1280]{1,0:T(8,128)(2,1)}) custom-call(bf16[128,7168]{1,0:T(8,128)(2,1)} %li.1, s32[2,128]{1,0:T(2,128)} %bitcast.9, bf16[160,128]{1,0:T(8,128)(2,1)} %bitcast.8, bf16[160,7168]{1,0:T(8,128)(2,1)} %bitcast.5, bf16[768,1280]{1,0:T(8,128)(2,1)} %ecot_hbm.1, ...), custom_call_target="tpu_custom_call" | custom-call | tf_op jit(solution)/shard_map/pallas_call | solution.py:554
  128.3 1.6 %copy.16 = bf16[128,448]{0,1:T(8,128)(2,1)} copy(bf16[128,448]{0,1:T(8,128)(2,1)} %bitcast.6) | data formatting | bytes 229376
  129.8 1.5 %copy.17 = f32[112,160]{0,1:T(8,128)} copy(f32[112,160]{0,1:T(8,128)} %bitcast.7) | data formatting | bytes 143360
  131.4 2.3 %copy.18 = bf16[448,1280]{1,0:T(8,128)(2,1)} copy(bf16[448,1280]{1,0:T(8,128)(2,1)} %get-tuple-element.14) | data formatting | bytes 2293760

commit v5 on v4

--- a/solution.py
+++ b/solution.py
@@ -253,7 +253,7 @@
     def each_way(back, fn):
         @pl.loop(1, pairs)
         def _(i):
-            d = far_first(i)
+            d = pairs * (1 - i % 2) + (2 * (i % 2) - 1) * ((i + 1) // 2)
 
             @pl.when(goes_back(d) == back)
             def _():
@@ -328,30 +328,6 @@
     for h in range(nh):
         dacc[h * ny + y] = core_sum(h * ny + y)
 
-    @pl.when(zh == 0)
-    def _():
-        wait_higher_z()
-        send_rows(True)
-
-    def rz_copy(sp, k, slot):
-        return copy(rs.at[sp, k], rz.at[slot], rz_s.at[2 * k + sp], rz_r.at[slot], at_z(2 * k + sp))
-
-    def pair_sum(sp, k):
-        pe_copy(sp, k).wait_recv()
-        return (pz[sp, k].astype(F32) + pin[sp, k].astype(F32)).astype(BF16)
-
-    def return_rows(sp, k):
-        rs[sp, k] = pair_sum(sp, k)
-        rz_copy(sp, k, pair).start()
-
-    each_on(par, return_rows)
-    rz[pair] = pair_sum(par, pair)
-
-    @pl.when(zh == 0)
-    def _():
-        pl.semaphore_wait(higher_h, nz)
-        send_rows(False)
-
     def h_copy():
         return copy(hsend, hrecv, h_s.at[0], h_r.at[0], other_h)
 
@@ -364,7 +340,34 @@
         dacc[h * ny + y] = total
     hsend[...] = dacc[(1 - zh) * ny + y].astype(BF16)
 
-    h_copy().start()
+    @pl.when(zh == 1)
+    def _():
+        h_copy().start()
+
+    @pl.when(zh == 0)
+    def _():
+        wait_higher_z()
+        send_rows(True)
+
+    def rz_copy(sp, k, slot):
+        return copy(rs.at[sp, k], rz.at[slot], rz_s.at[2 * k + sp], rz_r.at[slot], at_z(2 * k + sp))
+
+    def pair_sum(sp, k):
+        pe_copy(sp, k).wait_recv()
+        return (pz[sp, k].astype(F32) + pin[sp, k].astype(F32)).astype(BF16)
+
+    def return_rows(sp, k):
+        rs[sp, k] = pair_sum(sp, k)
+        rz_copy(sp, k, pair).start()
+
+    each_on(par, return_rows)
+    rz[pair] = pair_sum(par, pair)
+
+    @pl.when(zh == 0)
+    def _():
+        pl.semaphore_wait(higher_h, nz)
+        h_copy().start()
+        send_rows(False)
 
     def wz_at(step):
         base, size = 0, nz

time: 134 us -> 142 us (1.060)
  the two profiles are of different devices: /device:TPU:5 before, /device:TPU:1 now
where the time goes in v5:
time: 142 us; the launch traced here: 140 us
  Pallas kernels  134 us (94%)
  local copies, waits for them, and re-layouts  5.41 us (4%)
    pallas_call x1, Pallas kernels, body(): pl.pallas_call(functools.partial(kernel, (nx, nz, ny, nh)), out_shape=(ja...  134 us
    unnamed x3, local copies, waits for them, and re-layouts  5.41 us

profile of v5, /device:TPU:1, one launch (start us, length us, event | category | flops | bytes accessed | tf_op | source)
XLA Modules:
  0.0 139.6 jit_solution(9317849106037123781)
XLA Ops:
  0.6 133.6 %shard_map.121 = (bf16[448,128]{1,0:T(8,128)(2,1)}, f32[160,112]{1,0:T(8,128)}, bf16[448,1280]{1,0:T(8,128)(2,1)}) custom-call(bf16[128,7168]{1,0:T(8,128)(2,1)} %li.1, s32[2,128]{1,0:T(2,128)} %bitcast.9, bf16[160,128]{1,0:T(8,128)(2,1)} %bitcast.8, bf16[160,7168]{1,0:T(8,128)(2,1)} %bitcast.5, bf16[768,1280]{1,0:T(8,128)(2,1)} %ecot_hbm.1, ...), custom_call_target="tpu_custom_call" | custom-call | tf_op jit(solution)/shard_map/pallas_call | solution.py:557
  134.2 1.6 %copy.16 = bf16[128,448]{0,1:T(8,128)(2,1)} copy(bf16[128,448]{0,1:T(8,128)(2,1)} %bitcast.6) | data formatting | bytes 229376
  135.8 1.5 %copy.17 = f32[112,160]{0,1:T(8,128)} copy(f32[112,160]{0,1:T(8,128)} %bitcast.7) | data formatting | bytes 143360
  137.3 2.3 %copy.18 = bf16[448,1280]{1,0:T(8,128)(2,1)} copy(bf16[448,1280]{1,0:T(8,128)(2,1)} %get-tuple-element.14) | data formatting | bytes 2293760
